TPU v7x, 128 devices: a whole 4x4x4 slice. The times are simulated.
128 devices in a mesh: seq: 128 (over x, z, y, core).
Axes of the slice: x: 4, y: 4, z: 4, core: 2. Of those that a mesh axis runs over, the one named last changes fastest.
Arguments:
- queries: bfloat16 [65536, 768], P('seq'), may hold values from -180 to 180
- keys: bfloat16 [65536, 768], P('seq'), may hold values from -6 to 6
- values: bfloat16 [65536, 768], P('seq'), may hold values from -6 to 6
- w_out: bfloat16 [768, 768], replicated, may hold values from -0.21875 to 0.21875
Outputs:
- layer_out: bfloat16 [65536, 768], P('seq')
All inputs are finite; a program needn't handle non-finite values.
Results may differ from a plain program's by a relative error of at most 0.0052.
Values may be sent and summed in bfloat16 or wider, within the bound.
A program may use at most 128 MiB of HBM per device.

v0:
```python
import functools

import jax
import jax.numpy as jnp
from jax import lax
from jax.experimental import pallas as pl
from jax.experimental.pallas import tpu as pltpu
from jax.sharding import PartitionSpec as P

ROWS = 512
D = 768
HEADS = 12
HD = 64
GROUPS = 3
PAIRS = 6
NEAR = 128
FAR = 16
REST = NEAR - FAR
WIDE = 2 * HD
NONE = -1e30
F32 = jnp.float32
BF16 = jnp.bfloat16
MESH = pl.DeviceIdType.MESH


T_PAIR, T_CROSS, T_X, T_SIB = 0, 1, 2, 3
P_CROSS, P_X, P_SIB = 4, 5, 6
C_X, C_SIB = 7, 8
D_X, D_SIB = 9, 10
X_SIB = 11
Q_UP, Q_DOWN, Q_FAR = 15, 16, 17
X4_SAME, X4_OTHER = 18, 19
R_DOWN, R_UP, R_FAR = 20, 21, 22
L2_PAIR, L2_SIB, L2_FWD = 23, 26, 29
COPIES = 32


def nt(a, b):
    return lax.dot_general(a, b, (((1,), (1,)), ((), ())), preferred_element_type=F32)


def nn(a, b):
    return jnp.dot(a, b, preferred_element_type=F32)


def iota(shape, dim):
    return lax.broadcasted_iota(jnp.int32, shape, dim)


def one_hot(hit):
    return jnp.where(hit, 1.0, 0.0).astype(BF16)


def kernel(
    q_hbm, k_hbm, v_hbm, w_hbm, out_hbm,
    qbuf, kbuf, vbuf, wbuf, pick, back, qp, vt, tg, kvr, qg, x4s, x4, rs, rg, rm, att, sa, sb, pa, pb, o1, m1, outbuf,
    local_sem, out_sem, send_sem, recv_sem,
):
    me = lax.axis_index("seq")
    zed = (me >> 3) & 3
    above = (me - (zed << 3)) + (((zed + 1) & 3) << 3)
    below = (me - (zed << 3)) + (((zed + 3) & 3) << 3)
    opposite = me ^ 16
    sib, pair, cross, xpeer, other, other_sib = me ^ 1, me ^ 2, me ^ 6, me ^ 32, me ^ 96, me ^ 97

    loads = []
    for number, (hbm, buf) in enumerate(((k_hbm, kbuf), (v_hbm, vbuf), (q_hbm, qbuf), (w_hbm, wbuf))):
        load = pltpu.make_async_copy(hbm, buf, local_sem.at[number])
        load.start()
        loads.append(load)
    barrier = pltpu.get_barrier_semaphore()
    peers = (sib, pair, cross, xpeer, other, other_sib, above, below)
    for peer in peers:
        pl.semaphore_signal(barrier, inc=1, device_id=(peer,), device_id_type=MESH)

    def copy(number, src, dst, device):
        return pltpu.make_async_remote_copy(
            src_ref=src, dst_ref=dst, send_sem=send_sem.at[number], recv_sem=recv_sem.at[number],
            device_id=(device,), device_id_type=MESH,
        )

    remote = {
        T_PAIR: copy(T_PAIR, tg.at[0], tg.at[1], pair),
        T_CROSS: copy(T_CROSS, tg.at[0], tg.at[4], cross),
        T_X: copy(T_X, tg.at[0], tg.at[8], xpeer),
        T_SIB: copy(T_SIB, tg.at[0], tg.at[2], sib),
        P_CROSS: copy(P_CROSS, tg.at[1], tg.at[5], cross),
        P_X: copy(P_X, tg.at[1], tg.at[9], xpeer),
        P_SIB: copy(P_SIB, tg.at[1], tg.at[3], sib),
        C_X: copy(C_X, tg.at[4], tg.at[12], xpeer),
        C_SIB: copy(C_SIB, tg.at[4], tg.at[6], sib),
        D_X: copy(D_X, tg.at[5], tg.at[13], xpeer),
        D_SIB: copy(D_SIB, tg.at[5], tg.at[7], sib),
        Q_UP: copy(Q_UP, qg.at[0], qg.at[1], above),
        Q_DOWN: copy(Q_DOWN, qg.at[0], qg.at[2], below),
        Q_FAR: copy(Q_FAR, qg.at[1], qg.at[3], above),
        X4_SAME: copy(X4_SAME, x4s, x4.at[0], other),
        X4_OTHER: copy(X4_OTHER, x4s, x4.at[1], other_sib),
        R_DOWN: copy(R_DOWN, rs.at[1], rg.at[2], below),
        R_UP: copy(R_UP, rs.at[2], rg.at[1], above),
        R_FAR: copy(R_FAR, rs.at[3], rg.at[3], opposite),
    }
    for step, slot in enumerate((8, 9, 12, 13)):
        remote[X_SIB + step] = copy(X_SIB + step, tg.at[slot], tg.at[slot + 2], sib)
    for group in range(GROUPS):
        heads = pl.ds(4 * group, 4)
        remote[L2_PAIR + group] = copy(L2_PAIR + group, kvr.at[0, heads], kvr.at[1, heads], pair)
        remote[L2_SIB + group] = copy(L2_SIB + group, kvr.at[0, heads], kvr.at[2, heads], sib)
        remote[L2_FWD + group] = copy(L2_FWD + group, kvr.at[1, heads], kvr.at[3, heads], sib)

    def start(*numbers):
        for number in numbers:
            remote[number].start()

    def arrived(*numbers):
        for number in numbers:
            remote[number].wait_recv()

    place = iota((ROWS, NEAR), 0)
    position = ((place & 1) << 8) + (((place >> 1) & 7) << 5) + (((place >> 4) & 7) << 2) + (place >> 7)
    column = iota((ROWS, NEAR), 1)
    for c in range(4):
        pick[:, NEAR * c : NEAR * c + NEAR] = one_hot(column + NEAR * c == position)

    low_lanes = iota((NEAR, WIDE), 1) < HD

    loads[0].wait()
    loads[1].wait()
    for t in range(PAIRS):
        b, r = t // 2, 2 * (t % 2)
        columns = pl.ds(WIDE * t, WIDE)
        rows = pick[NEAR * r : NEAR * r + 2 * NEAR, :]
        both = nn(rows, jnp.concatenate((kbuf[:, columns], vbuf[:, columns]), axis=1))
        for kind in range(2):
            lanes = slice(WIDE * kind, WIDE * kind + WIDE)
            rows = jnp.where(low_lanes, both[:NEAR, lanes], both[NEAR:, lanes]).astype(BF16)
            tg[0, 2 * t + kind] = rows[FAR * b : FAR * b + FAR]
            if b > 0:
                kvr[0, 2 * t + kind, 0 : FAR * b, :] = rows[: FAR * b]
            kvr[0, 2 * t + kind, FAR * b : REST, :] = rows[FAR * b + FAR :]
    pl.semaphore_wait(barrier, len(peers))
    start(T_PAIR, T_CROSS, T_X, T_SIB, L2_PAIR)

    loads[2].wait()
    wide_low = iota((ROWS, WIDE), 1) < HD
    for b in range(GROUPS):
        ordered = nn(pick[...], qbuf[:, 256 * b : 256 * b + 256]) * 0.125
        for r in range(4):
            part = ordered[:, 128 * (r // 2) : 128 * (r // 2) + 128]
            part = jnp.where(wide_low, *((0.0, part) if r % 2 else (part, 0.0))).astype(BF16)
            qp[4 * b + r] = part
            qg[0, 4 * b + r] = part[NEAR * r + FAR * b : NEAR * r + FAR * b + FAR]
    start(Q_UP, Q_DOWN, L2_PAIR + 1, L2_PAIR + 2, L2_SIB, L2_SIB + 1, L2_SIB + 2)

    eye = one_hot(iota((WIDE, WIDE), 0) == iota((WIDE, WIDE), 1))

    for t in range(PAIRS):
        vt[WIDE * t : WIDE * t + WIDE, :] = nt(eye, vbuf[:, WIDE * t : WIDE * t + WIDE]).astype(BF16)
    ones = jnp.ones((FAR, ROWS), BF16)

    def scores_of(j, part, into):
        columns = pl.ds(pl.multiple_of((j >> 1) * WIDE, WIDE), WIDE)
        span = pl.ds(256 * part, 256)
        scores = nt(kbuf[:, columns], qp[j, span, :])
        into[...] = scores
        m1[j, :, span] = jnp.broadcast_to(jnp.max(scores, axis=0, keepdims=True), (8, 256))

    def weights_of(j, part, scores, into):
        highest = m1[j, 0:1, 256 * part : 256 * part + 256]
        into[...] = jnp.exp(scores[...] - highest).astype(BF16)

    def mixed_of(j, part, weights):
        span = pl.ds(256 * part, 256)
        left = jnp.concatenate((vt[pl.ds(pl.multiple_of(j * HD, HD), HD), :], ones), axis=0)
        mixed = nn(left, weights[...])
        att[pl.ds(pl.multiple_of(j * HD, HD), HD), span] = (mixed[:HD] * (1.0 / mixed[HD : HD + 1])).astype(BF16)
        o1[j, :, span] = mixed

    def level_ones(first, last):
        def step(j, carry):
            weights_of(j, 0, sa, pa)
            scores_of(j, 1, sb)
            mixed_of(jnp.maximum(j - 1, 0), 1, pb)
            weights_of(j, 1, sb, pb)
            scores_of(jnp.minimum(j + 1, HEADS - 1), 0, sa)
            mixed_of(j, 0, pa)
            return carry

        lax.fori_loop(first, last, step, 0)

    def level_two(group):
        heads = [(t, e) for t in (2 * group, 2 * group + 1) for e in range(2)]
        keys, turned, scores, highs, weights = {}, {}, {}, {}, {}

        def whole(entry):
            return jnp.concatenate(
                (tg[0:4, entry].reshape(4 * FAR, WIDE), kvr[0:4, entry].reshape(4 * REST, WIDE)), axis=0
            )

        def prepare(t):
            keys[t] = whole(2 * t)
            turned[t] = nt(eye, whole(2 * t + 1)).astype(BF16)

        def score(t, e):
            j = 2 * t + e
            scores[j] = nt(keys[t], qp[j, NEAR * (j % 4) : NEAR * (j % 4) + NEAR, :])

        def weigh(t, e):
            j = 2 * t + e
            highs[j] = jnp.max(scores[j], axis=0, keepdims=True)
            weights[j] = jnp.exp(scores[j] - highs[j]).astype(BF16)

        def mix(t, e):
            j = 2 * t + e
            mixed = nn(jnp.concatenate((turned[t][HD * e : HD * e + HD], ones), axis=0), weights[j])
            block = pl.ds(NEAR * (j % 4), NEAR)
            before = m1[j, 0:1, block]
            newest = jnp.maximum(before, highs[j])
            o1[j, :, block] = o1[j, :, block] * jnp.exp(before - newest) + mixed * jnp.exp(highs[j] - newest)
            m1[j, :, block] = jnp.broadcast_to(newest, (8, NEAR))

        for i in range(len(heads) + 2):
            if i < len(heads):
                if heads[i][1] == 0:
                    prepare(heads[i][0])
                score(*heads[i])
            if 0 <= i - 1 < len(heads):
                weigh(*heads[i - 1])
            if 0 <= i - 2 < len(heads):
                mix(*heads[i - 2])

    def compact():
        rows = iota((FAR, 8 * FAR), 0)
        picked = one_hot(iota((FAR, 8 * FAR), 1) == (rows >> 1) * FAR + (rows & 1))
        for entry in range(HEADS):
            tiles = jnp.concatenate([tg[slot, entry] for slot in (0, 1, 4, 5, 8, 9, 12, 13)], axis=0)
            x4s[entry] = nn(picked, tiles).astype(BF16)

    def partials():
        row = iota((4 * FAR, 16 * FAR), 0)
        col = iota((4 * FAR, 16 * FAR), 1)
        bias = jnp.where(((row & 15) < 2) & ((col & 15) < 2), 0.6931471805599453, 0.0).astype(F32)
        member = (iota((4 * FAR, 2 * FAR), 0) & 15) < 2
        low = iota((4 * FAR, WIDE), 1) < HD
        first_half = iota((4 * FAR, WIDE), 1) < HD + HD // 2
        heads = range(HEADS)
        far = [tg[:, entry].reshape(16 * FAR, WIDE) for entry in heads]
        off = [x4[:, entry].reshape(2 * FAR, WIDE) for entry in heads]
        keys3, values3 = [far[j - j % 2] for j in heads], [far[j - j % 2 + 1] for j in heads]
        keys4, values4 = [off[j - j % 2] for j in heads], [off[j - j % 2 + 1] for j in heads]
        queries = [qg[:, j].reshape(4 * FAR, WIDE) for j in heads]
        scores3 = [nt(queries[j], keys3[j]) + bias for j in heads]
        scores4 = [jnp.where(member, nt(queries[j], keys4[j]), NONE) for j in heads]
        highest = [
            jnp.maximum(
                jnp.max(scores3[j], axis=1, keepdims=True), jnp.max(scores4[j], axis=1, keepdims=True)
            )
            for j in heads
        ]
        weights3 = [jnp.exp(scores3[j] - highest[j]) for j in heads]
        weights4 = [jnp.exp(scores4[j] - highest[j]) for j in heads]
        totals = [
            jnp.sum(weights3[j], axis=1, keepdims=True) + jnp.sum(weights4[j], axis=1, keepdims=True)
            for j in heads
        ]
        mixed = [nn(weights3[j].astype(BF16), values3[j]) + nn(weights4[j].astype(BF16), values4[j]) for j in heads]
        for j in heads:
            value = mixed[j] * (1.0 / totals[j])
            if j % 2 == 1:
                value = pltpu.roll(value, HD, 1)
            level = highest[j] + jnp.log(totals[j])
            coarse = level.astype(BF16).astype(F32)
            fine = level - coarse
            whole = jnp.where(low, value, jnp.where(first_half, coarse, fine)).astype(BF16)
            for slot in range(4):
                rs[slot, j] = whole[FAR * slot : FAR * slot + FAR]

    def merge_partials():
        rows = HEADS * FAR
        low = iota((rows, WIDE), 1) < HD
        source = iota((WIDE, WIDE), 0)
        gather = one_hot((source == HD) | (source == HD + HD // 2))
        tiles = [rs[0].reshape(rows, WIDE)] + [rg[slot].reshape(rows, WIDE) for slot in (1, 2, 3)]
        levels = [nn(tile, gather) for tile in tiles]
        highest = functools.reduce(jnp.maximum, levels)
        factors = [jnp.exp(level - highest) for level in levels]
        total = functools.reduce(jnp.add, factors)
        value = functools.reduce(jnp.add, [f * t.astype(F32) for f, t in zip(factors, tiles)])
        merged = jnp.where(low, value / total, highest + jnp.log(total))
        rm[...] = merged.reshape(HEADS, FAR, WIDE)

    def finish(j):
        b, r = j // 4, j % 4
        empty = jnp.where(iota((REST, WIDE), 1) < HD, 0.0, NONE).astype(F32)
        rows = (rm[j], empty) if b == 0 else (empty[: FAR * b], rm[j], empty[FAR * b :])
        far = jnp.concatenate(rows, axis=0).T
        block = pl.ds(NEAR * r, NEAR)
        level = far[HD : HD + 1]
        before = m1[j, 0:1, block]
        newest = jnp.maximum(before, level)
        old, new = jnp.exp(before - newest), jnp.exp(level - newest)
        whole = o1[j, :, block]
        total = whole[HD : HD + 1] * old + new
        value = (whole[:HD] * old + far[:HD] * new) * (1.0 / total)
        att[HD * j : HD * j + HD, block] = value.astype(BF16)

    pb[...] = jnp.zeros_like(pb)
    scores_of(0, 0, sa)
    level_ones(0, 1)
    arrived(T_PAIR)
    start(P_CROSS, P_X, P_SIB)
    level_ones(1, 2)
    arrived(T_CROSS)
    start(C_X, C_SIB)
    arrived(Q_UP)
    start(Q_FAR)
    level_ones(2, 4)
    arrived(P_CROSS)
    start(D_X, D_SIB)
    arrived(T_X, P_X)
    start(X_SIB, X_SIB + 1)
    level_ones(4, 6)
    arrived(L2_PAIR)
    start(L2_FWD)
    arrived(C_X, D_X)
    start(X_SIB + 2, X_SIB + 3)
    compact()
    start(X4_SAME, X4_OTHER)
    level_ones(6, 10)
    arrived(L2_PAIR + 1)
    start(L2_FWD + 1)
    arrived(T_SIB, P_SIB, C_SIB, D_SIB, X_SIB, X_SIB + 1, X_SIB + 2, X_SIB + 3)
    arrived(Q_DOWN, Q_FAR, X4_SAME, X4_OTHER)
    partials()
    start(R_DOWN, R_UP, R_FAR)
    level_ones(10, 12)
    mixed_of(HEADS - 1, 1, pb)
    spot = iota((ROWS, NEAR), 0)
    index = ((spot & 3) << 7) + (((spot >> 2) & 7) << 4) + (((spot >> 5) & 7) << 1) + (spot >> 8)
    column = iota((ROWS, NEAR), 1)
    for c in range(4):
        back[:, NEAR * c : NEAR * c + NEAR] = one_hot(column + NEAR * c == index)
    arrived(L2_SIB, L2_FWD)
    level_two(0)
    arrived(L2_PAIR + 2)
    start(L2_FWD + 2)
    arrived(L2_SIB + 1, L2_FWD + 1)
    level_two(1)
    arrived(L2_SIB + 2, L2_FWD + 2)
    level_two(2)
    arrived(R_DOWN, R_UP, R_FAR)
    merge_partials()
    for j in range(HEADS):
        finish(j)
    loads[3].wait()
    natural = nt(back[...], att[...]).astype(BF16)
    outbuf[...] = nn(natural, wbuf[...]).astype(BF16)
    store = pltpu.make_async_copy(outbuf, out_hbm, out_sem)
    store.start()
    for number in range(COPIES):
        remote[number].wait_send()
    store.wait()


def body(queries, keys, values, w_out):
    anywhere = pl.BlockSpec(memory_space=pltpu.HBM)
    scratch = [
        pltpu.VMEM((ROWS, D), BF16),
        pltpu.VMEM((ROWS, D), BF16),
        pltpu.VMEM((ROWS, D), BF16),
        pltpu.VMEM((D, D), BF16),
        pltpu.VMEM((ROWS, ROWS), BF16),
        pltpu.VMEM((ROWS, ROWS), BF16),
        pltpu.VMEM((HEADS, ROWS, WIDE), BF16),
        pltpu.VMEM((D, ROWS), BF16),
        pltpu.VMEM((16, HEADS, FAR, WIDE), BF16),
        pltpu.VMEM((4, HEADS, REST, WIDE), BF16),
        pltpu.VMEM((4, HEADS, FAR, WIDE), BF16),
        pltpu.VMEM((HEADS, FAR, WIDE), BF16),
        pltpu.VMEM((2, HEADS, FAR, WIDE), BF16),
        pltpu.VMEM((4, HEADS, FAR, WIDE), BF16),
        pltpu.VMEM((4, HEADS, FAR, WIDE), BF16),
        pltpu.VMEM((HEADS, FAR, WIDE), F32),
        pltpu.VMEM((D, ROWS), BF16),
        pltpu.VMEM((ROWS, 256), F32),
        pltpu.VMEM((ROWS, 256), F32),
        pltpu.VMEM((ROWS, 256), BF16),
        pltpu.VMEM((ROWS, 256), BF16),
        pltpu.VMEM((HEADS, HD + FAR, ROWS), F32),
        pltpu.VMEM((HEADS, 8, ROWS), F32),
        pltpu.VMEM((ROWS, D), BF16),
        pltpu.SemaphoreType.DMA((4,)),
        pltpu.SemaphoreType.DMA,
        pltpu.SemaphoreType.DMA((COPIES,)),
        pltpu.SemaphoreType.DMA((COPIES,)),
    ]
    return pl.pallas_call(
        kernel,
        out_shape=jax.ShapeDtypeStruct((ROWS, D), BF16),
        in_specs=[anywhere] * 4,
        out_specs=anywhere,
        scratch_shapes=scratch,
        compiler_params=pltpu.CompilerParams(
            collective_id=0, has_side_effects=True, vmem_limit_bytes=53760 * 1024
        ),
        name="dilated_attention",
    )(queries, keys, values, w_out)


def solution(mesh):
    return jax.shard_map(
        body,
        mesh=mesh,
        in_specs=(P("seq", None), P("seq", None), P("seq", None), P()),
        out_specs=P("seq", None),
        check_vma=False,
    )
```

profile of v0, /device:TPU:1, one launch (start us, length us, event | category | flops | bytes accessed | tf_op | source)
XLA Modules:
  0.0 30.6 jit_solution(13591360750614464949)
XLA Ops:
  0.0 29.7 %dilated_attention.1 = bf16[512,768]{1,0:T(8,128)(2,1)S(1)} custom-call(bf16[512,768]{1,0:T(8,128)(2,1)} %q_hbm.1, bf16[512,768]{1,0:T(8,128)(2,1)} %k_hbm.1, bf16[512,768]{1,0:T(8,128)(2,1)} %v_hbm.1, bf16[768,768]{1,0:T(8,128)(2,1)} %w_hbm.1), custom_call_target="tpu_custom_call" | custom-call | tf_op jit(solution)/shard_map/dilated_attention/pallas_call | solution.py:397
  29.7 0.9 %copy.6 = bf16[512,768]{1,0:T(8,128)(2,1)} copy(bf16[512,768]{1,0:T(8,128)(2,1)S(1)} %dilated_attention.1) | data formatting | bytes 1572864
where the time goes:
time: 30.7 us; the launch traced here: 30.6 us
  Pallas kernels  29.7 us (97%)
  local copies, waits for them, and re-layouts  0.88 us (3%)
    pallas_call x1, Pallas kernels, body(): pl.pallas_call(kernel, out_shape=jax.ShapeDtypeStruct((ROWS, D), BF16), i...  29.7 us
    unnamed x1, local copies, waits for them, and re-layouts  0.88 us

commit v1 on v0

--- a/solution.py
+++ b/solution.py
@@ -23,16 +23,13 @@
 MESH = pl.DeviceIdType.MESH
 
 
-T_PAIR, T_CROSS, T_X, T_SIB = 0, 1, 2, 3
-P_CROSS, P_X, P_SIB = 4, 5, 6
-C_X, C_SIB = 7, 8
-D_X, D_SIB = 9, 10
-X_SIB = 11
-Q_UP, Q_DOWN, Q_FAR = 15, 16, 17
-X4_SAME, X4_OTHER = 18, 19
-R_DOWN, R_UP, R_FAR = 20, 21, 22
-L2_PAIR, L2_SIB, L2_FWD = 23, 26, 29
-COPIES = 32
+T_SEND = 0
+T_FORWARD = 4
+Q_SEND = 7
+X_SEND = 14
+R_SEND = 22
+L2_PAIR, L2_SIB, L2_FWD = 29, 32, 35
+COPIES = 38
 
 
 def nt(a, b):
@@ -58,10 +55,14 @@
 ):
     me = lax.axis_index("seq")
     zed = (me >> 3) & 3
-    above = (me - (zed << 3)) + (((zed + 1) & 3) << 3)
-    below = (me - (zed << 3)) + (((zed + 3) & 3) << 3)
-    opposite = me ^ 16
-    sib, pair, cross, xpeer, other, other_sib = me ^ 1, me ^ 2, me ^ 6, me ^ 32, me ^ 96, me ^ 97
+    sib, pair = me ^ 1, me ^ 2
+    base = me - (zed << 3)
+
+    def around(slot):
+        return (base + (((zed + slot) & 3) << 3)) ^ ((slot >> 2) << 5)
+
+    def reverse(slot):
+        return (slot & 4) + ((4 - slot) & 3)
 
     loads = []
     for number, (hbm, buf) in enumerate(((k_hbm, kbuf), (v_hbm, vbuf), (q_hbm, qbuf), (w_hbm, wbuf))):
@@ -69,7 +70,7 @@
         load.start()
         loads.append(load)
     barrier = pltpu.get_barrier_semaphore()
-    peers = (sib, pair, cross, xpeer, other, other_sib, above, below)
+    peers = [sib] + [me ^ (2 * s) for s in (1, 2, 3)] + [around(s) for s in range(1, 8)] + [me ^ (96 + s) for s in range(8)]
     for peer in peers:
         pl.semaphore_signal(barrier, inc=1, device_id=(peer,), device_id_type=MESH)
 
@@ -79,29 +80,17 @@
             device_id=(device,), device_id_type=MESH,
         )
 
-    remote = {
-        T_PAIR: copy(T_PAIR, tg.at[0], tg.at[1], pair),
-        T_CROSS: copy(T_CROSS, tg.at[0], tg.at[4], cross),
-        T_X: copy(T_X, tg.at[0], tg.at[8], xpeer),
-        T_SIB: copy(T_SIB, tg.at[0], tg.at[2], sib),
-        P_CROSS: copy(P_CROSS, tg.at[1], tg.at[5], cross),
-        P_X: copy(P_X, tg.at[1], tg.at[9], xpeer),
-        P_SIB: copy(P_SIB, tg.at[1], tg.at[3], sib),
-        C_X: copy(C_X, tg.at[4], tg.at[12], xpeer),
-        C_SIB: copy(C_SIB, tg.at[4], tg.at[6], sib),
-        D_X: copy(D_X, tg.at[5], tg.at[13], xpeer),
-        D_SIB: copy(D_SIB, tg.at[5], tg.at[7], sib),
-        Q_UP: copy(Q_UP, qg.at[0], qg.at[1], above),
-        Q_DOWN: copy(Q_DOWN, qg.at[0], qg.at[2], below),
-        Q_FAR: copy(Q_FAR, qg.at[1], qg.at[3], above),
-        X4_SAME: copy(X4_SAME, x4s, x4.at[0], other),
-        X4_OTHER: copy(X4_OTHER, x4s, x4.at[1], other_sib),
-        R_DOWN: copy(R_DOWN, rs.at[1], rg.at[2], below),
-        R_UP: copy(R_UP, rs.at[2], rg.at[1], above),
-        R_FAR: copy(R_FAR, rs.at[3], rg.at[3], opposite),
-    }
-    for step, slot in enumerate((8, 9, 12, 13)):
-        remote[X_SIB + step] = copy(X_SIB + step, tg.at[slot], tg.at[slot + 2], sib)
+    remote = {}
+    for step, (mask, slot) in enumerate(((2, 1), (6, 4), (4, 5), (1, 2))):
+        remote[T_SEND + step] = copy(T_SEND + step, tg.at[0], tg.at[slot], me ^ mask)
+    for step, slot in enumerate((1, 4, 5)):
+        remote[T_FORWARD + step] = copy(T_FORWARD + step, tg.at[slot], tg.at[slot + 2], sib)
+    for slot in range(1, 8):
+        number = slot - 1
+        remote[Q_SEND + number] = copy(Q_SEND + number, qg.at[0], qg.at[reverse(slot)], around(slot))
+        remote[R_SEND + number] = copy(R_SEND + number, rs.at[slot], rg.at[reverse(slot)], around(slot))
+    for slot in range(8):
+        remote[X_SEND + slot] = copy(X_SEND + slot, x4s, x4.at[slot], me ^ (96 + slot))
     for group in range(GROUPS):
         heads = pl.ds(4 * group, 4)
         remote[L2_PAIR + group] = copy(L2_PAIR + group, kvr.at[0, heads], kvr.at[1, heads], pair)
@@ -138,8 +127,9 @@
             if b > 0:
                 kvr[0, 2 * t + kind, 0 : FAR * b, :] = rows[: FAR * b]
             kvr[0, 2 * t + kind, FAR * b : REST, :] = rows[FAR * b + FAR :]
-    pl.semaphore_wait(barrier, len(peers))
-    start(T_PAIR, T_CROSS, T_X, T_SIB, L2_PAIR)
+    compact = iota((2 * FAR, HEADS * FAR), 0)
+    compact = one_hot(iota((2 * FAR, HEADS * FAR), 1) == (compact >> 1) * FAR + (compact & 1))
+    x4s[...] = nn(compact, tg[0].reshape(HEADS * FAR, WIDE)).astype(BF16)
 
     loads[2].wait()
     wide_low = iota((ROWS, WIDE), 1) < HD
@@ -147,10 +137,15 @@
         ordered = nn(pick[...], qbuf[:, 256 * b : 256 * b + 256]) * 0.125
         for r in range(4):
             part = ordered[:, 128 * (r // 2) : 128 * (r // 2) + 128]
-            part = jnp.where(wide_low, *((0.0, part) if r % 2 else (part, 0.0))).astype(BF16)
-            qp[4 * b + r] = part
-            qg[0, 4 * b + r] = part[NEAR * r + FAR * b : NEAR * r + FAR * b + FAR]
-    start(Q_UP, Q_DOWN, L2_PAIR + 1, L2_PAIR + 2, L2_SIB, L2_SIB + 1, L2_SIB + 2)
+            whole = part[NEAR * r + FAR * b : NEAR * r + FAR * b + FAR]
+            if r % 2 == 0:
+                before = whole
+            else:
+                qg[0, 2 * b + r // 2] = jnp.where(low_lanes[:FAR], before, whole).astype(BF16)
+            qp[4 * b + r] = jnp.where(wide_low, *((0.0, part) if r % 2 else (part, 0.0))).astype(BF16)
+    pl.semaphore_wait(barrier, len(peers))
+    start(*range(T_SEND, T_SEND + 3), *range(Q_SEND, Q_SEND + 7), *range(X_SEND, X_SEND + 8))
+    start(L2_PAIR, L2_PAIR + 1, L2_PAIR + 2, T_SEND + 3, L2_SIB, L2_SIB + 1, L2_SIB + 2)
 
     eye = one_hot(iota((WIDE, WIDE), 0) == iota((WIDE, WIDE), 1))
 
@@ -229,111 +224,110 @@
             if 0 <= i - 2 < len(heads):
                 mix(*heads[i - 2])
 
-    def compact():
-        rows = iota((FAR, 8 * FAR), 0)
-        picked = one_hot(iota((FAR, 8 * FAR), 1) == (rows >> 1) * FAR + (rows & 1))
-        for entry in range(HEADS):
-            tiles = jnp.concatenate([tg[slot, entry] for slot in (0, 1, 4, 5, 8, 9, 12, 13)], axis=0)
-            x4s[entry] = nn(picked, tiles).astype(BF16)
-
     def partials():
-        row = iota((4 * FAR, 16 * FAR), 0)
-        col = iota((4 * FAR, 16 * FAR), 1)
-        bias = jnp.where(((row & 15) < 2) & ((col & 15) < 2), 0.6931471805599453, 0.0).astype(F32)
-        member = (iota((4 * FAR, 2 * FAR), 0) & 15) < 2
-        low = iota((4 * FAR, WIDE), 1) < HD
-        first_half = iota((4 * FAR, WIDE), 1) < HD + HD // 2
-        heads = range(HEADS)
-        far = [tg[:, entry].reshape(16 * FAR, WIDE) for entry in heads]
-        off = [x4[:, entry].reshape(2 * FAR, WIDE) for entry in heads]
-        keys3, values3 = [far[j - j % 2] for j in heads], [far[j - j % 2 + 1] for j in heads]
-        keys4, values4 = [off[j - j % 2] for j in heads], [off[j - j % 2 + 1] for j in heads]
-        queries = [qg[:, j].reshape(4 * FAR, WIDE) for j in heads]
-        scores3 = [nt(queries[j], keys3[j]) + bias for j in heads]
-        scores4 = [jnp.where(member, nt(queries[j], keys4[j]), NONE) for j in heads]
-        highest = [
-            jnp.maximum(
-                jnp.max(scores3[j], axis=1, keepdims=True), jnp.max(scores4[j], axis=1, keepdims=True)
+        rows, near = 8 * FAR, (8 + 1) * FAR
+        order = iota((HEADS * FAR, 8 * 2 * FAR), 0)
+        column = iota((HEADS * FAR, 8 * 2 * FAR), 1)
+        wanted = ((order & 15) >> 1) * 2 * FAR + (order >> 4) * 2 + (order & 1)
+        other = nn(one_hot(column == wanted), x4[...].reshape(8 * 2 * FAR, WIDE)).astype(BF16)
+        row, col = iota((near, rows), 0), iota((near, rows), 1)
+        own_half = row < rows
+        member = (col & 15) < 2
+        bias = jnp.where(
+            own_half,
+            jnp.where(member & ((row & 15) < 2), 0.6931471805599453, 0.0),
+            jnp.where(member, 0.0, NONE),
+        ).astype(F32)
+        low = (iota((rows, WIDE), 1) < HD).astype(F32)
+        masks = (low.astype(BF16), (1.0 - low).astype(BF16))
+        ones = jnp.ones((FAR, near), BF16)
+        pairs, heads = range(PAIRS), range(HEADS)
+
+        def whole(entry):
+            return jnp.concatenate(
+                (tg[:, entry].reshape(rows, WIDE), other[FAR * entry : FAR * entry + FAR]), axis=0
             )
+
+        keys = [whole(2 * t) for t in pairs]
+        turned = [nt(eye, whole(2 * t + 1)).astype(BF16) for t in pairs]
+        queries = [qg[:, t].reshape(rows, WIDE) for t in pairs]
+        scores = [nt(keys[j // 2], queries[j // 2] * masks[j % 2]) + bias for j in heads]
+        highest = [jnp.max(scores[j], axis=0, keepdims=True) for j in heads]
+        weights = [jnp.exp(scores[j] - highest[j]).astype(BF16) for j in heads]
+        mixed = [
+            nn(jnp.concatenate((turned[j // 2][HD * (j % 2) : HD * (j % 2) + HD], ones), axis=0), weights[j])
             for j in heads
         ]
-        weights3 = [jnp.exp(scores3[j] - highest[j]) for j in heads]
-        weights4 = [jnp.exp(scores4[j] - highest[j]) for j in heads]
-        totals = [
-            jnp.sum(weights3[j], axis=1, keepdims=True) + jnp.sum(weights4[j], axis=1, keepdims=True)
-            for j in heads
-        ]
-        mixed = [nn(weights3[j].astype(BF16), values3[j]) + nn(weights4[j].astype(BF16), values4[j]) for j in heads]
-        for j in heads:
-            value = mixed[j] * (1.0 / totals[j])
-            if j % 2 == 1:
-                value = pltpu.roll(value, HD, 1)
-            level = highest[j] + jnp.log(totals[j])
-            coarse = level.astype(BF16).astype(F32)
-            fine = level - coarse
-            whole = jnp.where(low, value, jnp.where(first_half, coarse, fine)).astype(BF16)
-            for slot in range(4):
-                rs[slot, j] = whole[FAR * slot : FAR * slot + FAR]
+        totals = [mixed[j][HD : HD + 1] for j in heads]
+        values = [(mixed[j][:HD] * (1.0 / totals[j])).astype(BF16) for j in heads]
+        for t in pairs:
+            both = jnp.concatenate((values[2 * t], values[2 * t + 1]), axis=0)
+            rs[:, t] = nt(eye, both).astype(BF16).reshape(8, FAR, WIDE)
+        levels = [highest[j] + jnp.log(totals[j]) for j in heads]
+        levels = jnp.concatenate(levels + [jnp.zeros((4, rows), F32)], axis=0)
+        coarse = levels.astype(BF16)
+        fine = (levels - coarse.astype(F32)).astype(BF16)
+        stacked = jnp.concatenate((coarse, fine, jnp.zeros((WIDE - 2 * FAR, rows), BF16)), axis=0)
+        rs[:, PAIRS] = nt(eye, stacked).astype(BF16).reshape(8, FAR, WIDE)
 
     def merge_partials():
-        rows = HEADS * FAR
-        low = iota((rows, WIDE), 1) < HD
-        source = iota((WIDE, WIDE), 0)
-        gather = one_hot((source == HD) | (source == HD + HD // 2))
-        tiles = [rs[0].reshape(rows, WIDE)] + [rg[slot].reshape(rows, WIDE) for slot in (1, 2, 3)]
-        levels = [nn(tile, gather) for tile in tiles]
+        source, lane = iota((WIDE, D), 0), iota((WIDE, D), 1)
+        gather = one_hot(((source & 15) == (lane >> 6)) & (source < 2 * FAR))
+        rs_own = rs[0]
+        tiles = [rs_own] + [rg[slot] for slot in range(1, 8)]
+        values = [jnp.concatenate([tile[t] for t in range(PAIRS)], axis=1).astype(F32) for tile in tiles]
+        levels = nn(jnp.concatenate([tile[PAIRS] for tile in tiles], axis=0), gather)
+        levels = [levels[FAR * slot : FAR * slot + FAR] for slot in range(8)]
         highest = functools.reduce(jnp.maximum, levels)
         factors = [jnp.exp(level - highest) for level in levels]
         total = functools.reduce(jnp.add, factors)
-        value = functools.reduce(jnp.add, [f * t.astype(F32) for f, t in zip(factors, tiles)])
-        merged = jnp.where(low, value / total, highest + jnp.log(total))
-        rm[...] = merged.reshape(HEADS, FAR, WIDE)
+        value = functools.reduce(jnp.add, [f * v for f, v in zip(factors, values)]) / total
+        level = highest + jnp.log(total)
+        coarse = level.astype(BF16)
+        fine = (level - coarse.astype(F32)).astype(BF16)
+        value = value.astype(BF16)
+        column = iota((WIDE, NEAR), 1)
+        for t in range(PAIRS):
+            b = t // 2
+            lanes = slice(WIDE * t, WIDE * t + WIDE)
+
+            def spread(rows):
+                empty = jnp.zeros((REST, WIDE), BF16)
+                rows = (rows, empty) if b == 0 else (empty[: FAR * b], rows, empty[FAR * b :])
+                return nt(eye, jnp.concatenate(rows, axis=0))
+
+            rm[2 * t] = spread(value[:, lanes])
+            rm[2 * t + 1] = jnp.where(
+                (column >> 4) == b, spread(coarse[:, lanes]) + spread(fine[:, lanes]), NONE
+            )
 
     def finish(j):
-        b, r = j // 4, j % 4
-        empty = jnp.where(iota((REST, WIDE), 1) < HD, 0.0, NONE).astype(F32)
-        rows = (rm[j], empty) if b == 0 else (empty[: FAR * b], rm[j], empty[FAR * b :])
-        far = jnp.concatenate(rows, axis=0).T
+        r, rows = j % 4, HD * (j % 2)
         block = pl.ds(NEAR * r, NEAR)
-        level = far[HD : HD + 1]
+        level = rm[j - j % 2 + 1, rows : rows + 1, :]
         before = m1[j, 0:1, block]
         newest = jnp.maximum(before, level)
         old, new = jnp.exp(before - newest), jnp.exp(level - newest)
         whole = o1[j, :, block]
         total = whole[HD : HD + 1] * old + new
-        value = (whole[:HD] * old + far[:HD] * new) * (1.0 / total)
+        value = (whole[:HD] * old + rm[j - j % 2, rows : rows + HD, :] * new) * (1.0 / total)
         att[HD * j : HD * j + HD, block] = value.astype(BF16)
 
     pb[...] = jnp.zeros_like(pb)
     scores_of(0, 0, sa)
-    level_ones(0, 1)
-    arrived(T_PAIR)
-    start(P_CROSS, P_X, P_SIB)
-    level_ones(1, 2)
-    arrived(T_CROSS)
-    start(C_X, C_SIB)
-    arrived(Q_UP)
-    start(Q_FAR)
-    level_ones(2, 4)
-    arrived(P_CROSS)
-    start(D_X, D_SIB)
-    arrived(T_X, P_X)
-    start(X_SIB, X_SIB + 1)
+    level_ones(0, 4)
+    arrived(T_SEND, T_SEND + 1, T_SEND + 2)
+    start(T_FORWARD, T_FORWARD + 1, T_FORWARD + 2)
     level_ones(4, 6)
+    arrived(T_SEND + 3, *range(T_FORWARD, T_FORWARD + 3), *range(Q_SEND, Q_SEND + 7), *range(X_SEND, X_SEND + 8))
+    partials()
+    start(*range(R_SEND, R_SEND + 7))
     arrived(L2_PAIR)
     start(L2_FWD)
-    arrived(C_X, D_X)
-    start(X_SIB + 2, X_SIB + 3)
-    compact()
-    start(X4_SAME, X4_OTHER)
-    level_ones(6, 10)
+    level_ones(6, 9)
     arrived(L2_PAIR + 1)
     start(L2_FWD + 1)
-    arrived(T_SIB, P_SIB, C_SIB, D_SIB, X_SIB, X_SIB + 1, X_SIB + 2, X_SIB + 3)
-    arrived(Q_DOWN, Q_FAR, X4_SAME, X4_OTHER)
-    partials()
-    start(R_DOWN, R_UP, R_FAR)
-    level_ones(10, 12)
+    level_ones(9, 12)
     mixed_of(HEADS - 1, 1, pb)
     spot = iota((ROWS, NEAR), 0)
     index = ((spot & 3) << 7) + (((spot >> 2) & 7) << 4) + (((spot >> 5) & 7) << 1) + (spot >> 8)
@@ -348,7 +342,7 @@
     level_two(1)
     arrived(L2_SIB + 2, L2_FWD + 2)
     level_two(2)
-    arrived(R_DOWN, R_UP, R_FAR)
+    arrived(*range(R_SEND, R_SEND + 7))
     merge_partials()
     for j in range(HEADS):
         finish(j)
@@ -373,14 +367,14 @@
         pltpu.VMEM((ROWS, ROWS), BF16),
         pltpu.VMEM((HEADS, ROWS, WIDE), BF16),
         pltpu.VMEM((D, ROWS), BF16),
-        pltpu.VMEM((16, HEADS, FAR, WIDE), BF16),
+        pltpu.VMEM((8, HEADS, FAR, WIDE), BF16),
         pltpu.VMEM((4, HEADS, REST, WIDE), BF16),
-        pltpu.VMEM((4, HEADS, FAR, WIDE), BF16),
-        pltpu.VMEM((HEADS, FAR, WIDE), BF16),
-        pltpu.VMEM((2, HEADS, FAR, WIDE), BF16),
-        pltpu.VMEM((4, HEADS, FAR, WIDE), BF16),
-        pltpu.VMEM((4, HEADS, FAR, WIDE), BF16),
-        pltpu.VMEM((HEADS, FAR, WIDE), F32),
+        pltpu.VMEM((8, PAIRS, FAR, WIDE), BF16),
+        pltpu.VMEM((2 * FAR, WIDE), BF16),
+        pltpu.VMEM((8, 2 * FAR, WIDE), BF16),
+        pltpu.VMEM((8, PAIRS + 1, FAR, WIDE), BF16),
+        pltpu.VMEM((8, PAIRS + 1, FAR, WIDE), BF16),
+        pltpu.VMEM((HEADS, WIDE, NEAR), F32),
         pltpu.VMEM((D, ROWS), BF16),
         pltpu.VMEM((ROWS, 256), F32),
         pltpu.VMEM((ROWS, 256), F32),

time: 30.7 us -> 25.2 us (0.82)
  Pallas kernels: 29.7 us -> 24.2 us
    pallas_call x1, Pallas kernels: 29.7 us -> 24.2 us  [body(): pl.pallas_call(kernel, out_shape=jax.ShapeDtypeStruct((ROWS, D), BF16), i...]
where the time goes in v1:
time: 25.2 us; the launch traced here: 25.1 us
  Pallas kernels  24.2 us (96%)
  local copies, waits for them, and re-layouts  0.88 us (3%)
    pallas_call x1, Pallas kernels, body(): pl.pallas_call(kernel, out_shape=jax.ShapeDtypeStruct((ROWS, D), BF16), i...  24.2 us
    unnamed x1, local copies, waits for them, and re-layouts  0.88 us

profile of v1, /device:TPU:1, one launch (start us, length us, event | category | flops | bytes accessed | tf_op | source)
XLA Modules:
  0.0 25.1 jit_solution(16549944135480197651)
XLA Ops:
  0.0 24.2 %dilated_attention.1 = bf16[512,768]{1,0:T(8,128)(2,1)S(1)} custom-call(bf16[512,768]{1,0:T(8,128)(2,1)} %q_hbm.1, bf16[512,768]{1,0:T(8,128)(2,1)} %k_hbm.1, bf16[512,768]{1,0:T(8,128)(2,1)} %v_hbm.1, bf16[768,768]{1,0:T(8,128)(2,1)} %w_hbm.1), custom_call_target="tpu_custom_call" | custom-call | tf_op jit(solution)/shard_map/dilated_attention/pallas_call | solution.py:391
  24.2 0.9 %copy.6 = bf16[512,768]{1,0:T(8,128)(2,1)} copy(bf16[512,768]{1,0:T(8,128)(2,1)S(1)} %dilated_attention.1) | data formatting | bytes 1572864

commit v2 on v1

--- a/solution.py
+++ b/solution.py
@@ -28,8 +28,9 @@
 Q_SEND = 7
 X_SEND = 14
 R_SEND = 22
-L2_PAIR, L2_SIB, L2_FWD = 29, 32, 35
+L2_SIB, L2_PAIR, L2_FWD = 29, 30, 34
 COPIES = 38
+CHUNKS = ((0, 2), (2, 4), (4, 5), (5, 6))
 
 
 def nt(a, b):
@@ -49,9 +50,9 @@
 
 
 def kernel(
-    q_hbm, k_hbm, v_hbm, w_hbm, out_hbm,
-    qbuf, kbuf, vbuf, wbuf, pick, back, qp, vt, tg, kvr, qg, x4s, x4, rs, rg, rm, att, sa, sb, pa, pb, o1, m1, outbuf,
-    local_sem, out_sem, send_sem, recv_sem,
+    q_hbm, k_hbm, v_hbm, w_hbm, out_ref,
+    qbuf, kbuf, vbuf, wbuf, pick, back, qp, vt, tg, kvr, qg, x4s, x4, rs, rg, rm, att, sa, sb, pa, pb, o1, m1,
+    local_sem, send_sem, recv_sem,
 ):
     me = lax.axis_index("seq")
     zed = (me >> 3) & 3
@@ -91,11 +92,11 @@
         remote[R_SEND + number] = copy(R_SEND + number, rs.at[slot], rg.at[reverse(slot)], around(slot))
     for slot in range(8):
         remote[X_SEND + slot] = copy(X_SEND + slot, x4s, x4.at[slot], me ^ (96 + slot))
-    for group in range(GROUPS):
-        heads = pl.ds(4 * group, 4)
-        remote[L2_PAIR + group] = copy(L2_PAIR + group, kvr.at[0, heads], kvr.at[1, heads], pair)
-        remote[L2_SIB + group] = copy(L2_SIB + group, kvr.at[0, heads], kvr.at[2, heads], sib)
-        remote[L2_FWD + group] = copy(L2_FWD + group, kvr.at[1, heads], kvr.at[3, heads], sib)
+    remote[L2_SIB] = copy(L2_SIB, kvr.at[0], kvr.at[2], sib)
+    for number, (first, last) in enumerate(CHUNKS):
+        entries = pl.ds(2 * first, 2 * (last - first))
+        remote[L2_PAIR + number] = copy(L2_PAIR + number, kvr.at[0, entries], kvr.at[1, entries], pair)
+        remote[L2_FWD + number] = copy(L2_FWD + number, kvr.at[1, entries], kvr.at[3, entries], sib)
 
     def start(*numbers):
         for number in numbers:
@@ -143,26 +144,33 @@
             else:
                 qg[0, 2 * b + r // 2] = jnp.where(low_lanes[:FAR], before, whole).astype(BF16)
             qp[4 * b + r] = jnp.where(wide_low, *((0.0, part) if r % 2 else (part, 0.0))).astype(BF16)
-    pl.semaphore_wait(barrier, len(peers))
-    start(*range(T_SEND, T_SEND + 3), *range(Q_SEND, Q_SEND + 7), *range(X_SEND, X_SEND + 8))
-    start(L2_PAIR, L2_PAIR + 1, L2_PAIR + 2, T_SEND + 3, L2_SIB, L2_SIB + 1, L2_SIB + 2)
-
     eye = one_hot(iota((WIDE, WIDE), 0) == iota((WIDE, WIDE), 1))
-
     for t in range(PAIRS):
         vt[WIDE * t : WIDE * t + WIDE, :] = nt(eye, vbuf[:, WIDE * t : WIDE * t + WIDE]).astype(BF16)
     ones = jnp.ones((FAR, ROWS), BF16)
 
+    pl.semaphore_wait(barrier, len(peers))
+    start(*range(T_SEND, T_SEND + 3), *range(Q_SEND, Q_SEND + 7), *range(X_SEND, X_SEND + 8))
+    start(*range(L2_PAIR, L2_PAIR + 4), T_SEND + 3, L2_SIB)
+
+
     def scores_of(j, part, into):
         columns = pl.ds(pl.multiple_of((j >> 1) * WIDE, WIDE), WIDE)
         span = pl.ds(256 * part, 256)
-        scores = nt(kbuf[:, columns], qp[j, span, :])
-        into[...] = scores
-        m1[j, :, span] = jnp.broadcast_to(jnp.max(scores, axis=0, keepdims=True), (8, 256))
+        queries = qp[j, span, :]
+        highest = None
+        for c in range(4):
+            scores = nt(kbuf[NEAR * c : NEAR * c + NEAR, columns], queries)
+            into[NEAR * c : NEAR * c + NEAR, :] = scores
+            top = jnp.max(scores.reshape(16, 8, 256), axis=0)
+            highest = top if highest is None else jnp.maximum(highest, top)
+        m1[j, :, span] = jnp.broadcast_to(jnp.max(highest, axis=0, keepdims=True), (8, 256))
 
     def weights_of(j, part, scores, into):
         highest = m1[j, 0:1, 256 * part : 256 * part + 256]
-        into[...] = jnp.exp(scores[...] - highest).astype(BF16)
+        for c in range(4):
+            rows = slice(NEAR * c, NEAR * c + NEAR)
+            into[rows, :] = jnp.exp(scores[rows, :] - highest).astype(BF16)
 
     def mixed_of(j, part, weights):
         span = pl.ds(256 * part, 256)
@@ -183,8 +191,8 @@
 
         lax.fori_loop(first, last, step, 0)
 
-    def level_two(group):
-        heads = [(t, e) for t in (2 * group, 2 * group + 1) for e in range(2)]
+    def level_two(chunk):
+        heads = [(t, e) for t in range(*CHUNKS[chunk]) for e in range(2)]
         keys, turned, scores, highs, weights = {}, {}, {}, {}, {}
 
         def whole(entry):
@@ -315,21 +323,24 @@
 
     pb[...] = jnp.zeros_like(pb)
     scores_of(0, 0, sa)
-    level_ones(0, 4)
-    arrived(T_SEND, T_SEND + 1, T_SEND + 2)
-    start(T_FORWARD, T_FORWARD + 1, T_FORWARD + 2)
-    level_ones(4, 6)
-    arrived(T_SEND + 3, *range(T_FORWARD, T_FORWARD + 3), *range(Q_SEND, Q_SEND + 7), *range(X_SEND, X_SEND + 8))
+    level_ones(0, 6)
+    arrived(T_SEND)
+    start(T_FORWARD)
+    arrived(T_SEND + 1, T_SEND + 2)
+    start(T_FORWARD + 1, T_FORWARD + 2)
+    level_ones(6, 10)
+    arrived(*range(Q_SEND, Q_SEND + 7), T_SEND + 3, *range(T_FORWARD, T_FORWARD + 3), *range(X_SEND, X_SEND + 8))
     partials()
-    start(*range(R_SEND, R_SEND + 7))
+    start(*(R_SEND + slot - 1 for slot in (6, 2, 5, 7, 4, 1, 3)))
     arrived(L2_PAIR)
     start(L2_FWD)
-    level_ones(6, 9)
+    level_ones(10, 11)
     arrived(L2_PAIR + 1)
     start(L2_FWD + 1)
-    level_ones(9, 12)
+    level_ones(11, 12)
     mixed_of(HEADS - 1, 1, pb)
     spot = iota((ROWS, NEAR), 0)
+    spot = (((spot & 255) >> 4) << 5) + (spot & 15) + ((1 - (spot >> 8)) << 4)
     index = ((spot & 3) << 7) + (((spot >> 2) & 7) << 4) + (((spot >> 5) & 7) << 1) + (spot >> 8)
     column = iota((ROWS, NEAR), 1)
     for c in range(4):
@@ -338,22 +349,35 @@
     level_two(0)
     arrived(L2_PAIR + 2)
     start(L2_FWD + 2)
-    arrived(L2_SIB + 1, L2_FWD + 1)
+    arrived(L2_FWD + 1)
     level_two(1)
-    arrived(L2_SIB + 2, L2_FWD + 2)
+    arrived(L2_PAIR + 3)
+    start(L2_FWD + 3)
+    arrived(L2_FWD + 2)
     level_two(2)
+    arrived(L2_FWD + 3)
+    level_two(3)
+    for j in range(HEADS):
+        block = pl.ds(NEAR * (j % 4), NEAR)
+        whole = o1[j, :, block]
+        att[HD * j : HD * j + HD, block] = (whole[:HD] * (1.0 / whole[HD : HD + 1])).astype(BF16)
+
+    def project(part):
+        natural = nt(back[256 * part : 256 * part + 256, :], att[...]).astype(BF16)
+        rows = nn(natural, wbuf[...]).astype(BF16)
+        for m in range(16):
+            first = 32 * m + 16 - 16 * part
+            out_ref[first : first + 16, :] = rows[16 * m : 16 * m + 16]
+
+    loads[3].wait()
+    project(0)
     arrived(*range(R_SEND, R_SEND + 7))
     merge_partials()
     for j in range(HEADS):
         finish(j)
-    loads[3].wait()
-    natural = nt(back[...], att[...]).astype(BF16)
-    outbuf[...] = nn(natural, wbuf[...]).astype(BF16)
-    store = pltpu.make_async_copy(outbuf, out_hbm, out_sem)
-    store.start()
+    project(1)
     for number in range(COPIES):
         remote[number].wait_send()
-    store.wait()
 
 
 def body(queries, keys, values, w_out):
@@ -382,9 +406,7 @@
         pltpu.VMEM((ROWS, 256), BF16),
         pltpu.VMEM((HEADS, HD + FAR, ROWS), F32),
         pltpu.VMEM((HEADS, 8, ROWS), F32),
-        pltpu.VMEM((ROWS, D), BF16),
         pltpu.SemaphoreType.DMA((4,)),
-        pltpu.SemaphoreType.DMA,
         pltpu.SemaphoreType.DMA((COPIES,)),
         pltpu.SemaphoreType.DMA((COPIES,)),
     ]
@@ -392,7 +414,7 @@
         kernel,
         out_shape=jax.ShapeDtypeStruct((ROWS, D), BF16),
         in_specs=[anywhere] * 4,
-        out_specs=anywhere,
+        out_specs=pl.BlockSpec(memory_space=pltpu.VMEM),
         scratch_shapes=scratch,
         compiler_params=pltpu.CompilerParams(
             collective_id=0, has_side_effects=True, vmem_limit_bytes=53760 * 1024

time: 25.2 us -> 24.7 us (0.980)
  Pallas kernels: 24.2 us -> 23.7 us
    pallas_call x1, Pallas kernels: 24.2 us -> 23.7 us  [body(): pl.pallas_call(kernel, out_shape=jax.ShapeDtypeStruct((ROWS, D), BF16), i...]
where the time goes in v2:
time: 24.7 us; the launch traced here: 24.6 us
  Pallas kernels  23.7 us (96%)
  local copies, waits for them, and re-layouts  0.88 us (4%)
    pallas_call x1, Pallas kernels, body(): pl.pallas_call(kernel, out_shape=jax.ShapeDtypeStruct((ROWS, D), BF16), i...  23.7 us
    unnamed x1, local copies, waits for them, and re-layouts  0.88 us

profile of v2, /device:TPU:1, one launch (start us, length us, event | category | flops | bytes accessed | tf_op | source)
XLA Modules:
  0.0 24.6 jit_solution(2027960097986175991)
XLA Ops:
  0.0 23.7 %dilated_attention.1 = bf16[512,768]{1,0:T(8,128)(2,1)S(1)} custom-call(bf16[512,768]{1,0:T(8,128)(2,1)} %q_hbm.1, bf16[512,768]{1,0:T(8,128)(2,1)} %k_hbm.1, bf16[512,768]{1,0:T(8,128)(2,1)} %v_hbm.1, bf16[768,768]{1,0:T(8,128)(2,1)} %w_hbm.1), custom_call_target="tpu_custom_call" | custom-call | tf_op jit(solution)/shard_map/dilated_attention/pallas_call | solution.py:413
  23.7 0.9 %copy.6 = bf16[512,768]{1,0:T(8,128)(2,1)} copy(bf16[512,768]{1,0:T(8,128)(2,1)S(1)} %dilated_attention.1) | data formatting | bytes 1572864

commit v3 on v2

--- a/solution.py
+++ b/solution.py
@@ -28,9 +28,9 @@
 Q_SEND = 7
 X_SEND = 14
 R_SEND = 22
-L2_SIB, L2_PAIR, L2_FWD = 29, 30, 34
-COPIES = 38
-CHUNKS = ((0, 2), (2, 4), (4, 5), (5, 6))
+L2_SIB, L2_PAIR, L2_FWD = 29, 30, 33
+COPIES = 36
+CHUNKS = ((0, 2), (2, 4), (4, 6))
 
 
 def nt(a, b):
@@ -151,7 +151,7 @@
 
     pl.semaphore_wait(barrier, len(peers))
     start(*range(T_SEND, T_SEND + 3), *range(Q_SEND, Q_SEND + 7), *range(X_SEND, X_SEND + 8))
-    start(*range(L2_PAIR, L2_PAIR + 4), T_SEND + 3, L2_SIB)
+    start(*range(L2_PAIR, L2_PAIR + 3), T_SEND + 3, L2_SIB)
 
 
     def scores_of(j, part, into):
@@ -192,45 +192,55 @@
         lax.fori_loop(first, last, step, 0)
 
     def level_two(chunk):
-        heads = [(t, e) for t in range(*CHUNKS[chunk]) for e in range(2)]
-        keys, turned, scores, highs, weights = {}, {}, {}, {}, {}
+        pairs = range(*CHUNKS[chunk])
+        keys, lefts, highs = {}, {}, {}
+        held = {t: ((sa, pa), (sb, pb))[t % 2] for t in pairs}
 
         def whole(entry):
             return jnp.concatenate(
                 (tg[0:4, entry].reshape(4 * FAR, WIDE), kvr[0:4, entry].reshape(4 * REST, WIDE)), axis=0
             )
 
-        def prepare(t):
+        def score(t):
             keys[t] = whole(2 * t)
-            turned[t] = nt(eye, whole(2 * t + 1)).astype(BF16)
-
-        def score(t, e):
-            j = 2 * t + e
-            scores[j] = nt(keys[t], qp[j, NEAR * (j % 4) : NEAR * (j % 4) + NEAR, :])
-
-        def weigh(t, e):
-            j = 2 * t + e
-            highs[j] = jnp.max(scores[j], axis=0, keepdims=True)
-            weights[j] = jnp.exp(scores[j] - highs[j]).astype(BF16)
-
-        def mix(t, e):
-            j = 2 * t + e
-            mixed = nn(jnp.concatenate((turned[t][HD * e : HD * e + HD], ones), axis=0), weights[j])
-            block = pl.ds(NEAR * (j % 4), NEAR)
-            before = m1[j, 0:1, block]
-            newest = jnp.maximum(before, highs[j])
-            o1[j, :, block] = o1[j, :, block] * jnp.exp(before - newest) + mixed * jnp.exp(highs[j] - newest)
-            m1[j, :, block] = jnp.broadcast_to(newest, (8, NEAR))
-
-        for i in range(len(heads) + 2):
-            if i < len(heads):
-                if heads[i][1] == 0:
-                    prepare(heads[i][0])
-                score(*heads[i])
-            if 0 <= i - 1 < len(heads):
-                weigh(*heads[i - 1])
-            if 0 <= i - 2 < len(heads):
-                mix(*heads[i - 2])
+            queries = [qp[j, NEAR * (j % 4) : NEAR * (j % 4) + NEAR, :] for j in (2 * t, 2 * t + 1)]
+            queries = jnp.concatenate(queries, axis=0)
+            highest = None
+            for c in range(4):
+                rows = slice(NEAR * c, NEAR * c + NEAR)
+                scores = nt(keys[t][rows], queries)
+                held[t][0][rows, :] = scores
+                top = jnp.max(scores.reshape(16, 8, 256), axis=0)
+                highest = top if highest is None else jnp.maximum(highest, top)
+            highs[t] = jnp.max(highest, axis=0, keepdims=True)
+            lefts[t] = jnp.concatenate((nt(eye, whole(2 * t + 1)).astype(BF16), ones), axis=0)
+
+        def weigh(t):
+            for c in range(4):
+                rows = slice(NEAR * c, NEAR * c + NEAR)
+                held[t][1][rows, :] = jnp.exp(held[t][0][rows, :] - highs[t]).astype(BF16)
+
+        def mix(t):
+            both = nn(lefts[t], held[t][1][...])
+            for e in range(2):
+                j = 2 * t + e
+                lanes = slice(NEAR * e, NEAR * e + NEAR)
+                mixed = jnp.concatenate((both[HD * e : HD * e + HD, lanes], both[WIDE:, lanes]), axis=0)
+                highest = highs[t][:, lanes]
+                block = pl.ds(NEAR * (j % 4), NEAR)
+                before = m1[j, 0:1, block]
+                newest = jnp.maximum(before, highest)
+                o1[j, :, block] = o1[j, :, block] * jnp.exp(before - newest) + mixed * jnp.exp(highest - newest)
+                m1[j, :, block] = jnp.broadcast_to(newest, (8, NEAR))
+
+        pairs = list(pairs)
+        for i in range(len(pairs) + 2):
+            if i < len(pairs):
+                score(pairs[i])
+            if 0 <= i - 1 < len(pairs):
+                weigh(pairs[i - 1])
+            if 0 <= i - 2 < len(pairs):
+                mix(pairs[i - 2])
 
     def partials():
         rows, near = 8 * FAR, (8 + 1) * FAR
@@ -238,7 +248,7 @@
         column = iota((HEADS * FAR, 8 * 2 * FAR), 1)
         wanted = ((order & 15) >> 1) * 2 * FAR + (order >> 4) * 2 + (order & 1)
         other = nn(one_hot(column == wanted), x4[...].reshape(8 * 2 * FAR, WIDE)).astype(BF16)
-        row, col = iota((near, rows), 0), iota((near, rows), 1)
+        row, col = iota((near, 2 * rows), 0), iota((near, 2 * rows), 1)
         own_half = row < rows
         member = (col & 15) < 2
         bias = jnp.where(
@@ -248,7 +258,7 @@
         ).astype(F32)
         low = (iota((rows, WIDE), 1) < HD).astype(F32)
         masks = (low.astype(BF16), (1.0 - low).astype(BF16))
-        ones = jnp.ones((FAR, near), BF16)
+        beside = jnp.ones((FAR, near), BF16)
         pairs, heads = range(PAIRS), range(HEADS)
 
         def whole(entry):
@@ -257,21 +267,26 @@
             )
 
         keys = [whole(2 * t) for t in pairs]
-        turned = [nt(eye, whole(2 * t + 1)).astype(BF16) for t in pairs]
+        lefts = [jnp.concatenate((nt(eye, whole(2 * t + 1)).astype(BF16), beside), axis=0) for t in pairs]
         queries = [qg[:, t].reshape(rows, WIDE) for t in pairs]
-        scores = [nt(keys[j // 2], queries[j // 2] * masks[j % 2]) + bias for j in heads]
-        highest = [jnp.max(scores[j], axis=0, keepdims=True) for j in heads]
-        weights = [jnp.exp(scores[j] - highest[j]).astype(BF16) for j in heads]
-        mixed = [
-            nn(jnp.concatenate((turned[j // 2][HD * (j % 2) : HD * (j % 2) + HD], ones), axis=0), weights[j])
+        queries = [jnp.concatenate((q * masks[0], q * masks[1]), axis=0) for q in queries]
+        scores = [nt(keys[t], queries[t]) + bias for t in pairs]
+        highest = [jnp.max(scores[t], axis=0, keepdims=True) for t in pairs]
+        weights = [jnp.exp(scores[t] - highest[t]).astype(BF16) for t in pairs]
+        mixed = [nn(lefts[t], weights[t]) for t in pairs]
+        scales = [1.0 / mixed[t][WIDE : WIDE + 1] for t in pairs]
+        both_levels = [highest[t] + jnp.log(mixed[t][WIDE : WIDE + 1]) for t in pairs]
+        levels = [both_levels[j // 2][:, rows * (j % 2) : rows * (j % 2) + rows] for j in heads]
+        values = [
+            (
+                mixed[j // 2][HD * (j % 2) : HD * (j % 2) + HD, rows * (j % 2) : rows * (j % 2) + rows]
+                * scales[j // 2][:, rows * (j % 2) : rows * (j % 2) + rows]
+            ).astype(BF16)
             for j in heads
         ]
-        totals = [mixed[j][HD : HD + 1] for j in heads]
-        values = [(mixed[j][:HD] * (1.0 / totals[j])).astype(BF16) for j in heads]
         for t in pairs:
             both = jnp.concatenate((values[2 * t], values[2 * t + 1]), axis=0)
             rs[:, t] = nt(eye, both).astype(BF16).reshape(8, FAR, WIDE)
-        levels = [highest[j] + jnp.log(totals[j]) for j in heads]
         levels = jnp.concatenate(levels + [jnp.zeros((4, rows), F32)], axis=0)
         coarse = levels.astype(BF16)
         fine = (levels - coarse.astype(F32)).astype(BF16)
@@ -351,12 +366,8 @@
     start(L2_FWD + 2)
     arrived(L2_FWD + 1)
     level_two(1)
-    arrived(L2_PAIR + 3)
-    start(L2_FWD + 3)
     arrived(L2_FWD + 2)
     level_two(2)
-    arrived(L2_FWD + 3)
-    level_two(3)
     for j in range(HEADS):
         block = pl.ds(NEAR * (j % 4), NEAR)
         whole = o1[j, :, block]

time: 24.7 us -> 24.2 us (0.980)
  Pallas kernels: 23.7 us -> 23.2 us
    pallas_call x1, Pallas kernels: 23.7 us -> 23.2 us  [body(): pl.pallas_call(kernel, out_shape=jax.ShapeDtypeStruct((ROWS, D), BF16), i...]
where the time goes in v3:
time: 24.2 us; the launch traced here: 24.1 us
  Pallas kernels  23.2 us (96%)
  local copies, waits for them, and re-layouts  0.88 us (4%)
    pallas_call x1, Pallas kernels, body(): pl.pallas_call(kernel, out_shape=jax.ShapeDtypeStruct((ROWS, D), BF16), i...  23.2 us
    unnamed x1, local copies, waits for them, and re-layouts  0.88 us

profile of v3, /device:TPU:1, one launch (start us, length us, event | category | flops | bytes accessed | tf_op | source)
XLA Modules:
  0.0 24.1 jit_solution(10924881735352296052)
XLA Ops:
  0.0 23.2 %dilated_attention.1 = bf16[512,768]{1,0:T(8,128)(2,1)S(1)} custom-call(bf16[512,768]{1,0:T(8,128)(2,1)} %q_hbm.1, bf16[512,768]{1,0:T(8,128)(2,1)} %k_hbm.1, bf16[512,768]{1,0:T(8,128)(2,1)} %v_hbm.1, bf16[768,768]{1,0:T(8,128)(2,1)} %w_hbm.1), custom_call_target="tpu_custom_call" | custom-call | tf_op jit(solution)/shard_map/dilated_attention/pallas_call | solution.py:424
  23.2 0.9 %copy.6 = bf16[512,768]{1,0:T(8,128)(2,1)} copy(bf16[512,768]{1,0:T(8,128)(2,1)S(1)} %dilated_attention.1) | data formatting | bytes 1572864

commit v4 on v3

--- a/solution.py
+++ b/solution.py
@@ -242,12 +242,11 @@
             if 0 <= i - 2 < len(pairs):
                 mix(pairs[i - 2])
 
-    def partials():
+    def partial_constants():
         rows, near = 8 * FAR, (8 + 1) * FAR
         order = iota((HEADS * FAR, 8 * 2 * FAR), 0)
         column = iota((HEADS * FAR, 8 * 2 * FAR), 1)
         wanted = ((order & 15) >> 1) * 2 * FAR + (order >> 4) * 2 + (order & 1)
-        other = nn(one_hot(column == wanted), x4[...].reshape(8 * 2 * FAR, WIDE)).astype(BF16)
         row, col = iota((near, 2 * rows), 0), iota((near, 2 * rows), 1)
         own_half = row < rows
         member = (col & 15) < 2
@@ -259,6 +258,11 @@
         low = (iota((rows, WIDE), 1) < HD).astype(F32)
         masks = (low.astype(BF16), (1.0 - low).astype(BF16))
         beside = jnp.ones((FAR, near), BF16)
+        return one_hot(column == wanted), bias, masks, beside
+
+    def partials(wanted, bias, masks, beside):
+        rows = 8 * FAR
+        other = nn(wanted, x4[...].reshape(8 * 2 * FAR, WIDE)).astype(BF16)
         pairs, heads = range(PAIRS), range(HEADS)
 
         def whole(entry):
@@ -293,9 +297,11 @@
         stacked = jnp.concatenate((coarse, fine, jnp.zeros((WIDE - 2 * FAR, rows), BF16)), axis=0)
         rs[:, PAIRS] = nt(eye, stacked).astype(BF16).reshape(8, FAR, WIDE)
 
-    def merge_partials():
+    def level_lanes():
         source, lane = iota((WIDE, D), 0), iota((WIDE, D), 1)
-        gather = one_hot(((source & 15) == (lane >> 6)) & (source < 2 * FAR))
+        return one_hot(((source & 15) == (lane >> 6)) & (source < 2 * FAR))
+
+    def merge_partials(gather, member):
         rs_own = rs[0]
         tiles = [rs_own] + [rg[slot] for slot in range(1, 8)]
         values = [jnp.concatenate([tile[t] for t in range(PAIRS)], axis=1).astype(F32) for tile in tiles]
@@ -309,20 +315,16 @@
         coarse = level.astype(BF16)
         fine = (level - coarse.astype(F32)).astype(BF16)
         value = value.astype(BF16)
-        column = iota((WIDE, NEAR), 1)
+        empty = jnp.zeros((REST, WIDE), BF16)
         for t in range(PAIRS):
             b = t // 2
-            lanes = slice(WIDE * t, WIDE * t + WIDE)
-
-            def spread(rows):
-                empty = jnp.zeros((REST, WIDE), BF16)
-                rows = (rows, empty) if b == 0 else (empty[: FAR * b], rows, empty[FAR * b :])
-                return nt(eye, jnp.concatenate(rows, axis=0))
-
-            rm[2 * t] = spread(value[:, lanes])
-            rm[2 * t + 1] = jnp.where(
-                (column >> 4) == b, spread(coarse[:, lanes]) + spread(fine[:, lanes]), NONE
-            )
+            stack = []
+            for part in (value, coarse, fine):
+                part = part[:, WIDE * t : WIDE * t + WIDE]
+                stack += (part, empty) if b == 0 else (empty[: FAR * b], part, empty[FAR * b :])
+            spread = nt(eye, jnp.concatenate(stack, axis=0))
+            rm[2 * t] = spread[:, :NEAR]
+            rm[2 * t + 1] = jnp.where(member == b, spread[:, NEAR : 2 * NEAR] + spread[:, 2 * NEAR :], NONE)
 
     def finish(j):
         r, rows = j % 4, HD * (j % 2)
@@ -343,23 +345,23 @@
     start(T_FORWARD)
     arrived(T_SEND + 1, T_SEND + 2)
     start(T_FORWARD + 1, T_FORWARD + 2)
-    level_ones(6, 10)
-    arrived(*range(Q_SEND, Q_SEND + 7), T_SEND + 3, *range(T_FORWARD, T_FORWARD + 3), *range(X_SEND, X_SEND + 8))
-    partials()
-    start(*(R_SEND + slot - 1 for slot in (6, 2, 5, 7, 4, 1, 3)))
-    arrived(L2_PAIR)
-    start(L2_FWD)
-    level_ones(10, 11)
-    arrived(L2_PAIR + 1)
-    start(L2_FWD + 1)
-    level_ones(11, 12)
-    mixed_of(HEADS - 1, 1, pb)
+    level_ones(6, 11)
     spot = iota((ROWS, NEAR), 0)
     spot = (((spot & 255) >> 4) << 5) + (spot & 15) + ((1 - (spot >> 8)) << 4)
     index = ((spot & 3) << 7) + (((spot >> 2) & 7) << 4) + (((spot >> 5) & 7) << 1) + (spot >> 8)
     column = iota((ROWS, NEAR), 1)
     for c in range(4):
         back[:, NEAR * c : NEAR * c + NEAR] = one_hot(column + NEAR * c == index)
+    constants = partial_constants()
+    arrived(*range(Q_SEND, Q_SEND + 7), T_SEND + 3, *range(T_FORWARD, T_FORWARD + 3), *range(X_SEND, X_SEND + 8))
+    partials(*constants)
+    start(*(R_SEND + slot - 1 for slot in (6, 2, 5, 7, 4, 1, 3)))
+    arrived(L2_PAIR)
+    start(L2_FWD)
+    arrived(L2_PAIR + 1)
+    start(L2_FWD + 1)
+    level_ones(11, 12)
+    mixed_of(HEADS - 1, 1, pb)
     arrived(L2_SIB, L2_FWD)
     level_two(0)
     arrived(L2_PAIR + 2)
@@ -382,8 +384,9 @@
 
     loads[3].wait()
     project(0)
+    gather, member = level_lanes(), iota((WIDE, NEAR), 1) >> 4
     arrived(*range(R_SEND, R_SEND + 7))
-    merge_partials()
+    merge_partials(gather, member)
     for j in range(HEADS):
         finish(j)
     project(1)

time: 24.2 us -> 24.1 us (level)
  no operation moved by 1% of the time
where the time goes in v4:
time: 24.1 us; the launch traced here: 24 us
  Pallas kernels  23.1 us (96%)
  local copies, waits for them, and re-layouts  0.88 us (4%)
    pallas_call x1, Pallas kernels, body(): pl.pallas_call(kernel, out_shape=jax.ShapeDtypeStruct((ROWS, D), BF16), i...  23.1 us
    unnamed x1, local copies, waits for them, and re-layouts  0.88 us

profile of v4, /device:TPU:1, one launch (start us, length us, event | category | flops | bytes accessed | tf_op | source)
XLA Modules:
  0.0 24.0 jit_solution(3180299544173719206)
XLA Ops:
  0.0 23.1 %dilated_attention.1 = bf16[512,768]{1,0:T(8,128)(2,1)S(1)} custom-call(bf16[512,768]{1,0:T(8,128)(2,1)} %q_hbm.1, bf16[512,768]{1,0:T(8,128)(2,1)} %k_hbm.1, bf16[512,768]{1,0:T(8,128)(2,1)} %v_hbm.1, bf16[768,768]{1,0:T(8,128)(2,1)} %w_hbm.1), custom_call_target="tpu_custom_call" | custom-call | tf_op jit(solution)/shard_map/dilated_attention/pallas_call | solution.py:427
  23.1 0.9 %copy.6 = bf16[512,768]{1,0:T(8,128)(2,1)} copy(bf16[512,768]{1,0:T(8,128)(2,1)S(1)} %dilated_attention.1) | data formatting | bytes 1572864

commit v5 on v4

--- a/solution.py
+++ b/solution.py
@@ -145,14 +145,14 @@
                 qg[0, 2 * b + r // 2] = jnp.where(low_lanes[:FAR], before, whole).astype(BF16)
             qp[4 * b + r] = jnp.where(wide_low, *((0.0, part) if r % 2 else (part, 0.0))).astype(BF16)
     eye = one_hot(iota((WIDE, WIDE), 0) == iota((WIDE, WIDE), 1))
+    pl.semaphore_wait(barrier, len(peers))
+    start(*range(T_SEND, T_SEND + 3), *range(Q_SEND, Q_SEND + 7), *range(X_SEND, X_SEND + 8))
+    start(*range(L2_PAIR, L2_PAIR + 3), T_SEND + 3, L2_SIB)
+
+
     for t in range(PAIRS):
         vt[WIDE * t : WIDE * t + WIDE, :] = nt(eye, vbuf[:, WIDE * t : WIDE * t + WIDE]).astype(BF16)
     ones = jnp.ones((FAR, ROWS), BF16)
-
-    pl.semaphore_wait(barrier, len(peers))
-    start(*range(T_SEND, T_SEND + 3), *range(Q_SEND, Q_SEND + 7), *range(X_SEND, X_SEND + 8))
-    start(*range(L2_PAIR, L2_PAIR + 3), T_SEND + 3, L2_SIB)
-
 
     def scores_of(j, part, into):
         columns = pl.ds(pl.multiple_of((j >> 1) * WIDE, WIDE), WIDE)

time: 24.1 us -> 24.1 us (level)
  no operation moved by 1% of the time
where the time goes in v5:
time: 24.1 us; the launch traced here: 24 us
  Pallas kernels  23.1 us (96%)
  local copies, waits for them, and re-layouts  0.88 us (4%)
    pallas_call x1, Pallas kernels, body(): pl.pallas_call(kernel, out_shape=jax.ShapeDtypeStruct((ROWS, D), BF16), i...  23.1 us
    unnamed x1, local copies, waits for them, and re-layouts  0.88 us

profile of v5, /device:TPU:1, one launch (start us, length us, event | category | flops | bytes accessed | tf_op | source)
XLA Modules:
  0.0 24.0 jit_solution(6132624797050122643)
XLA Ops:
  0.0 23.1 %dilated_attention.1 = bf16[512,768]{1,0:T(8,128)(2,1)S(1)} custom-call(bf16[512,768]{1,0:T(8,128)(2,1)} %q_hbm.1, bf16[512,768]{1,0:T(8,128)(2,1)} %k_hbm.1, bf16[512,768]{1,0:T(8,128)(2,1)} %v_hbm.1, bf16[768,768]{1,0:T(8,128)(2,1)} %w_hbm.1), custom_call_target="tpu_custom_call" | custom-call | tf_op jit(solution)/shard_map/dilated_attention/pallas_call | solution.py:427
  23.1 0.9 %copy.6 = bf16[512,768]{1,0:T(8,128)(2,1)} copy(bf16[512,768]{1,0:T(8,128)(2,1)S(1)} %dilated_attention.1) | data formatting | bytes 1572864
